TPU v7x, 32 devices: a whole 2x2x4 slice. The times are simulated.
32 devices in a mesh: view: 4 (over y, x), brick: 8 (over z, core).
Axes of the slice: x: 2, y: 2, z: 4, core: 2. Of those that a mesh axis runs over, the one named last changes fastest.
Arguments:
- view_stacks: float32 [4, 128, 256, 256], P('view', 'brick'), may hold values from 0.2 to 5
- point_spread: float32 [4, 128, 256, 256], P('view', 'brick'), may hold values from 0 to 2, as said below
- weights_depth: float32 [4, 128, 128], P('view'), may hold values from 0 to 2, as said below
- weights_rows: float32 [4, 256, 256], P('view'), may hold values from 0 to 2, as said below
- weights_cols: float32 [4, 256, 256], P('view'), may hold values from 0 to 2, as said below
- depth_start: int32 [4, 256, 256], P('view'), may hold values from 0 to 63
- depth_stop: int32 [4, 256, 256], P('view'), may hold values from 65 to 128
Outputs:
- joined_brick: float32 [128, 256, 256], P('brick')
- deconvolved: float32 [128, 256, 256], P('brick')
Inputs may be any that keep to these rules, and one draw needn't show every extreme that they name: `point_spread`: nonnegative. `weights_depth`: nonnegative. `weights_rows`: nonnegative. `weights_cols`: nonnegative.
All inputs are finite; a program needn't handle non-finite values.
Results may differ from a plain program's by a relative error of at most 0.00012.
Values sent between devices are 32-bit elements; how exact they have to be, the bound alone decides.
A program may use at most 192 MiB of HBM per device.

v0:
```python
import math
import jax
import jax.numpy as jnp
from jax import lax
from jax.sharding import PartitionSpec as P

highest = lax.Precision.HIGHEST
einsum_forms = ("kyx,kj->jyx", "zkx,kj->zjx", "zyk,kj->zyj")


def dft_tables(length):
    counter = jnp.arange(length, dtype=jnp.int32)
    product = counter[:, None] * counter[None, :] % length
    angles = product.astype(jnp.float32) * (2.0 * math.pi / length)
    return (jnp.cos(angles), jnp.sin(angles))


def along_axis(values_in, table, axis_index):
    return jnp.einsum(einsum_forms[axis_index], values_in, table, precision=highest)


def forward_axis(real_part, imag_part, axis_index):
    cosine, sine = dft_tables(real_part.shape[axis_index])
    if imag_part is None:
        return (along_axis(real_part, cosine, axis_index), -along_axis(real_part, sine, axis_index))
    new_real = along_axis(real_part, cosine, axis_index) + along_axis(imag_part, sine, axis_index)
    new_imag = along_axis(imag_part, cosine, axis_index) - along_axis(real_part, sine, axis_index)
    return (new_real, new_imag)


def inverse_axis(real_part, imag_part, axis_index, real_only):
    length = real_part.shape[axis_index]
    cosine, sine = dft_tables(length)
    scale = 1.0 / length
    new_real = (
        along_axis(real_part, cosine, axis_index) - along_axis(imag_part, sine, axis_index)
    ) * scale
    if real_only:
        return new_real
    new_imag = (
        along_axis(imag_part, cosine, axis_index) + along_axis(real_part, sine, axis_index)
    ) * scale
    return (new_real, new_imag)


def resample_view(source, depth_map, row_map, col_map):
    across = jnp.einsum("zyx,ax->zya", source, col_map, precision=highest)
    across = jnp.einsum("zyx,by->zbx", across, row_map, precision=highest)
    mixed = jnp.einsum(
        "zyx,cz->cyx",
        lax.all_to_all(across, "brick", split_axis=1, concat_axis=0, tiled=True),
        depth_map,
        precision=highest,
    )
    return lax.all_to_all(mixed, "brick", split_axis=0, concat_axis=1, tiled=True)


def forward_transform(grid_values):
    real_part, imag_part = forward_axis(grid_values, None, 2)
    real_part, imag_part = forward_axis(real_part, imag_part, 1)
    depth_real, depth_imag = forward_axis(
        lax.all_to_all(real_part, "brick", split_axis=1, concat_axis=0, tiled=True),
        lax.all_to_all(imag_part, "brick", split_axis=1, concat_axis=0, tiled=True),
        0,
    )
    return (
        lax.all_to_all(depth_real, "brick", split_axis=0, concat_axis=1, tiled=True),
        lax.all_to_all(depth_imag, "brick", split_axis=0, concat_axis=1, tiled=True),
    )


def inverse_transform(real_part, imag_part):
    real_part, imag_part = (
        lax.all_to_all(real_part, "brick", split_axis=1, concat_axis=0, tiled=True),
        lax.all_to_all(imag_part, "brick", split_axis=1, concat_axis=0, tiled=True),
    )
    real_part, imag_part = inverse_axis(real_part, imag_part, 0, False)
    real_part, imag_part = inverse_axis(
        lax.all_to_all(real_part, "brick", split_axis=0, concat_axis=1, tiled=True),
        lax.all_to_all(imag_part, "brick", split_axis=0, concat_axis=1, tiled=True),
        1,
        False,
    )
    return inverse_axis(real_part, imag_part, 2, True)


def per_device(
    view_stacks, point_spread, weights_depth, weights_rows, weights_cols, depth_start, depth_stop
):
    resampled = resample_view(view_stacks[0], weights_depth[0], weights_rows[0], weights_cols[0])
    planes_here = resampled.shape[0]
    depth_index = lax.axis_index("brick") * planes_here + jnp.arange(planes_here, dtype=jnp.int32)
    depth_grid = depth_index[:, None, None]
    covered = jnp.logical_and(
        depth_grid >= depth_start[0][None], depth_grid < depth_stop[0][None]
    ).astype(jnp.float32)
    view_weight = 0.05 + covered * (1.0 + jnp.log(1.0 + resampled * resampled))
    weighted = view_weight * resampled
    total_signal, total_weight = lax.psum((weighted, view_weight), "view")
    joined_brick = total_signal / total_weight
    otf_real, otf_imag = forward_transform(point_spread[0])
    joined_real, joined_imag = forward_transform(joined_brick)
    blurred = inverse_transform(
        joined_real * otf_real - joined_imag * otf_imag,
        joined_real * otf_imag + joined_imag * otf_real,
    )
    ratio = resampled / blurred
    ratio_real, ratio_imag = forward_transform(ratio)
    correction = inverse_transform(
        ratio_real * otf_real + ratio_imag * otf_imag, ratio_imag * otf_real - ratio_real * otf_imag
    )
    correction_total = lax.psum(view_weight * correction, "view")
    deconvolved = joined_brick * correction_total / total_weight
    return (joined_brick, deconvolved)


def solution(mesh):
    return jax.shard_map(
        per_device,
        mesh=mesh,
        in_specs=(
            P("view", "brick", None, None),
            P("view", "brick", None, None),
            P("view", None, None),
            P("view", None, None),
            P("view", None, None),
            P("view", None, None),
            P("view", None, None),
        ),
        out_specs=(P("brick", None, None), P("brick", None, None)),
        check_vma=False,
    )
```

profile of v0, /device:TPU:0, one launch (start us, length us, event | category | flops | bytes accessed | tf_op | source)
XLA Modules:
  0.0 2484.0 jit_solution(6937730432940994262)
XLA Ops:
  69.3 55.4 %all-to-all-done = f32[16,256,256]{2,0,1:T(8,128)} async-done(((f32[16,256,256]{2,0,1:T(8,128)}), f32[16,256,256]{2,0,1:T(8,128)}, u32[]{:S(2)}, u32[]{:S(2)}) %all-to-all-start) | async-done | bytes 4194336 | tf_op jit(solution)/shard_map/all_to_all | solution.py:51
  148.7 74.5 %all-to-all-done.5 = f32[16,256,256]{2,0,1:T(8,128)} async-done(((f32[16,256,256]{2,0,1:T(8,128)}), f32[16,256,256]{2,0,1:T(8,128)}, u32[]{:S(2)}, u32[]{:S(2)}) %all-to-all-start.5) | async-done | bytes 4194336 | tf_op jit(solution)/shard_map/all_to_all | solution.py:62
  227.9 11.0 fusion.8
  251.0 70.8 %all-to-all-done.1 = f32[128,32,256]{2,1,0:T(8,128)} async-done(((f32[128,32,256]{2,1,0:T(8,128)}), f32[128,32,256]{2,1,0:T(8,128)}, u32[]{:S(2)}, u32[]{:S(2)}) %all-to-all-start.1) | async-done | bytes 4194336 | tf_op jit(solution)/shard_map/all_to_all | solution.py:55
  339.5 80.9 %all-to-all-done.6 = f32[16,256,256]{2,0,1:T(8,128)} async-done(((f32[16,256,256]{2,0,1:T(8,128)}), f32[16,256,256]{2,0,1:T(8,128)}, u32[]{:S(2)}, u32[]{:S(2)}) %all-to-all-start.6) | async-done | bytes 4194336 | tf_op jit(solution)/shard_map/all_to_all | solution.py:63
  440.6 68.1 %all-reduce.6.cloned.1.call-done = (f32[16,256,256]{2,1,0:T(8,128)}, f32[16,256,256]{2,1,0:T(8,128)}) async-done(((f32[16,256,256]{2,1,0:T(8,128)}, f32[16,256,256]{2,1,0:T(8,128)}), (f32[16,256,256]{2,1,0:T(8,128)}, f32[16,256,256]{2,1,0:T(8,128)})) %all-reduce.6.cloned.1.call-update) | async-done | bytes 8388624 | tf_op jit(solution)/shard_map/psum | solution.py:99
  558.1 77.5 %all-to-all-done.2 = f32[16,256,256]{2,0,1:T(8,128)} async-done(((f32[16,256,256]{2,0,1:T(8,128)}), f32[16,256,256]{2,0,1:T(8,128)}, u32[]{:S(2)}, u32[]{:S(2)}) %all-to-all-start.2) | async-done | bytes 4194336 | tf_op jit(solution)/shard_map/all_to_all | solution.py:62
  654.9 79.5 %all-to-all-done.3 = f32[16,256,256]{2,0,1:T(8,128)} async-done(((f32[16,256,256]{2,0,1:T(8,128)}), f32[16,256,256]{2,0,1:T(8,128)}, u32[]{:S(2)}, u32[]{:S(2)}) %all-to-all-start.3) | async-done | bytes 4194336 | tf_op jit(solution)/shard_map/all_to_all | solution.py:63
  759.1 74.3 %all-to-all-done.7 = f32[128,32,256]{2,1,0:T(8,128)} async-done(((f32[128,32,256]{2,1,0:T(8,128)}), f32[128,32,256]{2,1,0:T(8,128)}, u32[]{:S(2)}, u32[]{:S(2)}) %all-to-all-start.7) | async-done | bytes 4194336 | tf_op jit(solution)/shard_map/all_to_all | solution.py:67
  852.7 79.4 %all-to-all-done.8 = f32[128,32,256]{2,1,0:T(8,128)} async-done(((f32[128,32,256]{2,1,0:T(8,128)}), f32[128,32,256]{2,1,0:T(8,128)}, u32[]{:S(2)}, u32[]{:S(2)}) %all-to-all-start.8) | async-done | bytes 4194336 | tf_op jit(solution)/shard_map/all_to_all | solution.py:68
  932.1 97.9 %all_to_all.342 = f32[128,32,256]{2,1,0:T(8,128)S(1)} all-to-all(f32[128,32,256]{2,1,0:T(8,128)} %copy.158), channel_id=1, replica_groups=mesh['view'=4,'brick'=8] {'brick'}, dimensions={0} | all-to-all | bytes 8388608 | tf_op jit(solution)/shard_map/all_to_all | solution.py:67
  1059.1 87.0 %all-to-all-done.11 = f32[16,256,256]{2,0,1:T(8,128)} async-done(((f32[16,256,256]{2,0,1:T(8,128)}), f32[16,256,256]{2,0,1:T(8,128)}, u32[]{:S(2)}, u32[]{:S(2)}) %all-to-all-start.11) | async-done | bytes 4194336 | tf_op jit(solution)/shard_map/all_to_all | solution.py:75
  1155.8 89.2 %all-to-all-done.10 = f32[16,256,256]{2,0,1:T(8,128)} async-done(((f32[16,256,256]{2,0,1:T(8,128)}), f32[16,256,256]{2,0,1:T(8,128)}, u32[]{:S(2)}, u32[]{:S(2)}) %all-to-all-start.10) | async-done | bytes 4194336 | tf_op jit(solution)/shard_map/all_to_all | solution.py:74
  1280.8 79.3 %all-to-all-done.13 = f32[128,32,256]{2,1,0:T(8,128)} async-done(((f32[128,32,256]{2,1,0:T(8,128)}), f32[128,32,256]{2,1,0:T(8,128)}, u32[]{:S(2)}, u32[]{:S(2)}) %all-to-all-start.13) | async-done | bytes 4194336 | tf_op jit(solution)/shard_map/all_to_all | solution.py:80
  1381.7 76.9 %all-to-all-done.12 = f32[128,32,256]{2,1,0:T(8,128)} async-done(((f32[128,32,256]{2,1,0:T(8,128)}), f32[128,32,256]{2,1,0:T(8,128)}, u32[]{:S(2)}, u32[]{:S(2)}) %all-to-all-start.12) | async-done | bytes 4194336 | tf_op jit(solution)/shard_map/all_to_all | solution.py:79
  1525.6 77.4 %all-to-all-done.14 = f32[16,256,256]{2,0,1:T(8,128)} async-done(((f32[16,256,256]{2,0,1:T(8,128)}), f32[16,256,256]{2,0,1:T(8,128)}, u32[]{:S(2)}, u32[]{:S(2)}) %all-to-all-start.14) | async-done | bytes 4194336 | tf_op jit(solution)/shard_map/all_to_all | solution.py:62
  1612.5 89.2 %all-to-all-done.15 = f32[16,256,256]{2,0,1:T(8,128)} async-done(((f32[16,256,256]{2,0,1:T(8,128)}), f32[16,256,256]{2,0,1:T(8,128)}, u32[]{:S(2)}, u32[]{:S(2)}) %all-to-all-start.15) | async-done | bytes 4194336 | tf_op jit(solution)/shard_map/all_to_all | solution.py:63
  1736.6 79.5 %all-to-all-done.17 = f32[128,32,256]{2,1,0:T(8,128)} async-done(((f32[128,32,256]{2,1,0:T(8,128)}), f32[128,32,256]{2,1,0:T(8,128)}, u32[]{:S(2)}, u32[]{:S(2)}) %all-to-all-start.17) | async-done | bytes 4194336 | tf_op jit(solution)/shard_map/all_to_all | solution.py:68
  1816.1 97.8 %all_to_all.343 = f32[128,32,256]{2,1,0:T(8,128)S(1)} all-to-all(f32[128,32,256]{2,1,0:T(8,128)} %copy.200), channel_id=1, replica_groups=mesh['view'=4,'brick'=8] {'brick'}, dimensions={0} | all-to-all | bytes 8388608 | tf_op jit(solution)/shard_map/all_to_all | solution.py:67
  1942.9 87.1 %all-to-all-done.19 = f32[16,256,256]{2,0,1:T(8,128)} async-done(((f32[16,256,256]{2,0,1:T(8,128)}), f32[16,256,256]{2,0,1:T(8,128)}, u32[]{:S(2)}, u32[]{:S(2)}) %all-to-all-start.19) | async-done | bytes 4194336 | tf_op jit(solution)/shard_map/all_to_all | solution.py:75
  2039.6 89.1 %all-to-all-done.18 = f32[16,256,256]{2,0,1:T(8,128)} async-done(((f32[16,256,256]{2,0,1:T(8,128)}), f32[16,256,256]{2,0,1:T(8,128)}, u32[]{:S(2)}, u32[]{:S(2)}) %all-to-all-start.18) | async-done | bytes 4194336 | tf_op jit(solution)/shard_map/all_to_all | solution.py:74
  2164.7 79.2 %all-to-all-done.21 = f32[128,32,256]{2,1,0:T(8,128)} async-done(((f32[128,32,256]{2,1,0:T(8,128)}), f32[128,32,256]{2,1,0:T(8,128)}, u32[]{:S(2)}, u32[]{:S(2)}) %all-to-all-start.21) | async-done | bytes 4194336 | tf_op jit(solution)/shard_map/all_to_all | solution.py:80
  2265.4 77.1 %all-to-all-done.20 = f32[128,32,256]{2,1,0:T(8,128)} async-done(((f32[128,32,256]{2,1,0:T(8,128)}), f32[128,32,256]{2,1,0:T(8,128)}, u32[]{:S(2)}, u32[]{:S(2)}) %all-to-all-start.20) | async-done | bytes 4194336 | tf_op jit(solution)/shard_map/all_to_all | solution.py:79
  2366.7 102.6 %all-reduce.4.cloned.1.call-done = f32[16,256,256]{2,1,0:T(8,128)} async-done(((f32[16,256,256]{2,1,0:T(8,128)}), f32[16,256,256]{2,1,0:T(8,128)}) %all-reduce.4.cloned.1.call-update) | async-done | bytes 4194320 | tf_op jit(solution)/shard_map/psum | solution.py:112
  (203 shorter events, 588.0 us)
Async XLA Ops:
  24.3 100.4 %all-to-all-start = ((f32[16,256,256]{2,0,1:T(8,128)}), f32[16,256,256]{2,0,1:T(8,128)}, u32[]{:S(2)}, u32[]{:S(2)}) async-start(f32[16,256,256]{2,0,1:T(8,128)} %copy.144), calls=%async_computation | async-start | bytes 8388608 | tf_op jit(solution)/shard_map/all_to_all | solution.py:51
  41.3 15.7 copy-start.27
  124.7 98.6 %all-to-all-start.5 = ((f32[16,256,256]{2,0,1:T(8,128)}), f32[16,256,256]{2,0,1:T(8,128)}, u32[]{:S(2)}, u32[]{:S(2)}) async-start(f32[16,256,256]{2,0,1:T(8,128)} %copy.165), calls=%async_computation.5 | async-start | bytes 8388608 | tf_op jit(solution)/shard_map/all_to_all | solution.py:62
  223.3 98.6 %all-to-all-start.1 = ((f32[128,32,256]{2,1,0:T(8,128)}), f32[128,32,256]{2,1,0:T(8,128)}, u32[]{:S(2)}, u32[]{:S(2)}) async-start(f32[128,32,256]{2,1,0:T(8,128)} %copy.148), calls=%async_computation.1 | async-start | bytes 8388608 | tf_op jit(solution)/shard_map/all_to_all | solution.py:55
  227.8 11.0 copy-start.4
  321.8 98.6 %all-to-all-start.6 = ((f32[16,256,256]{2,0,1:T(8,128)}), f32[16,256,256]{2,0,1:T(8,128)}, u32[]{:S(2)}, u32[]{:S(2)}) async-start(f32[16,256,256]{2,0,1:T(8,128)} %copy.171), calls=%async_computation.6 | async-start | bytes 8388608 | tf_op jit(solution)/shard_map/all_to_all | solution.py:63
  326.4 182.2 %all-reduce.6.cloned.1.call-start = ((), (), s32[]{:S(2)}) async-start(), calls=%async_computation.23 | async-start | bytes 16777216 | tf_op jit(solution)/shard_map/psum | solution.py:99
  436.0 100.8 %all-to-all-start.9 = ((f32[128,32,256]{2,1,0:T(8,128)}), f32[128,32,256]{2,1,0:T(8,128)}, u32[]{:S(2)}, u32[]{:S(2)}) async-start(f32[128,32,256]{2,1,0:T(8,128)} %copy.175), calls=%async_computation.9 | async-start | bytes 8388608 | tf_op jit(solution)/shard_map/all_to_all | solution.py:68
  536.8 98.9 %all-to-all-start.2 = ((f32[16,256,256]{2,0,1:T(8,128)}), f32[16,256,256]{2,0,1:T(8,128)}, u32[]{:S(2)}, u32[]{:S(2)}) async-start(f32[16,256,256]{2,0,1:T(8,128)} %copy.152), calls=%async_computation.2 | async-start | bytes 8388608 | tf_op jit(solution)/shard_map/all_to_all | solution.py:62
  635.6 98.8 %all-to-all-start.3 = ((f32[16,256,256]{2,0,1:T(8,128)}), f32[16,256,256]{2,0,1:T(8,128)}, u32[]{:S(2)}, u32[]{:S(2)}) async-start(f32[16,256,256]{2,0,1:T(8,128)} %copy.156), calls=%async_computation.3 | async-start | bytes 8388608 | tf_op jit(solution)/shard_map/all_to_all | solution.py:63
  734.4 99.0 %all-to-all-start.7 = ((f32[128,32,256]{2,1,0:T(8,128)}), f32[128,32,256]{2,1,0:T(8,128)}, u32[]{:S(2)}, u32[]{:S(2)}) async-start(f32[128,32,256]{2,1,0:T(8,128)} %copy.173), calls=%async_computation.7 | async-start | bytes 8388608 | tf_op jit(solution)/shard_map/all_to_all | solution.py:67
  833.4 98.7 %all-to-all-start.8 = ((f32[128,32,256]{2,1,0:T(8,128)}), f32[128,32,256]{2,1,0:T(8,128)}, u32[]{:S(2)}, u32[]{:S(2)}) async-start(f32[128,32,256]{2,1,0:T(8,128)} %copy.174), calls=%async_computation.8 | async-start | bytes 8388608 | tf_op jit(solution)/shard_map/all_to_all | solution.py:68
  1047.4 98.6 %all-to-all-start.11 = ((f32[16,256,256]{2,0,1:T(8,128)}), f32[16,256,256]{2,0,1:T(8,128)}, u32[]{:S(2)}, u32[]{:S(2)}) async-start(f32[16,256,256]{2,0,1:T(8,128)} %copy.181), calls=%async_computation.11 | async-start | bytes 8388608 | tf_op jit(solution)/shard_map/all_to_all | solution.py:75
  1146.0 99.0 %all-to-all-start.10 = ((f32[16,256,256]{2,0,1:T(8,128)}), f32[16,256,256]{2,0,1:T(8,128)}, u32[]{:S(2)}, u32[]{:S(2)}) async-start(f32[16,256,256]{2,0,1:T(8,128)} %copy.177), calls=%async_computation.10 | async-start | bytes 8388608 | tf_op jit(solution)/shard_map/all_to_all | solution.py:74
  1261.3 98.8 %all-to-all-start.13 = ((f32[128,32,256]{2,1,0:T(8,128)}), f32[128,32,256]{2,1,0:T(8,128)}, u32[]{:S(2)}, u32[]{:S(2)}) async-start(f32[128,32,256]{2,1,0:T(8,128)} %copy.187), calls=%async_computation.13 | async-start | bytes 8388608 | tf_op jit(solution)/shard_map/all_to_all | solution.py:80
  1360.1 98.6 %all-to-all-start.12 = ((f32[128,32,256]{2,1,0:T(8,128)}), f32[128,32,256]{2,1,0:T(8,128)}, u32[]{:S(2)}, u32[]{:S(2)}) async-start(f32[128,32,256]{2,1,0:T(8,128)} %copy.184), calls=%async_computation.12 | async-start | bytes 8388608 | tf_op jit(solution)/shard_map/all_to_all | solution.py:79
  1504.3 98.6 %all-to-all-start.14 = ((f32[16,256,256]{2,0,1:T(8,128)}), f32[16,256,256]{2,0,1:T(8,128)}, u32[]{:S(2)}, u32[]{:S(2)}) async-start(f32[16,256,256]{2,0,1:T(8,128)} %copy.194), calls=%async_computation.14 | async-start | bytes 8388608 | tf_op jit(solution)/shard_map/all_to_all | solution.py:62
  1602.9 98.8 %all-to-all-start.15 = ((f32[16,256,256]{2,0,1:T(8,128)}), f32[16,256,256]{2,0,1:T(8,128)}, u32[]{:S(2)}, u32[]{:S(2)}) async-start(f32[16,256,256]{2,0,1:T(8,128)} %copy.198), calls=%async_computation.15 | async-start | bytes 8388608 | tf_op jit(solution)/shard_map/all_to_all | solution.py:63
  1717.1 99.0 %all-to-all-start.17 = ((f32[128,32,256]{2,1,0:T(8,128)}), f32[128,32,256]{2,1,0:T(8,128)}, u32[]{:S(2)}, u32[]{:S(2)}) async-start(f32[128,32,256]{2,1,0:T(8,128)} %copy.201), calls=%async_computation.17 | async-start | bytes 8388608 | tf_op jit(solution)/shard_map/all_to_all | solution.py:68
  1931.4 98.6 %all-to-all-start.19 = ((f32[16,256,256]{2,0,1:T(8,128)}), f32[16,256,256]{2,0,1:T(8,128)}, u32[]{:S(2)}, u32[]{:S(2)}) async-start(f32[16,256,256]{2,0,1:T(8,128)} %copy.207), calls=%async_computation.19 | async-start | bytes 8388608 | tf_op jit(solution)/shard_map/all_to_all | solution.py:75
  2030.0 98.8 %all-to-all-start.18 = ((f32[16,256,256]{2,0,1:T(8,128)}), f32[16,256,256]{2,0,1:T(8,128)}, u32[]{:S(2)}, u32[]{:S(2)}) async-start(f32[16,256,256]{2,0,1:T(8,128)} %copy.203), calls=%async_computation.18 | async-start | bytes 8388608 | tf_op jit(solution)/shard_map/all_to_all | solution.py:74
  2144.9 99.0 %all-to-all-start.21 = ((f32[128,32,256]{2,1,0:T(8,128)}), f32[128,32,256]{2,1,0:T(8,128)}, u32[]{:S(2)}, u32[]{:S(2)}) async-start(f32[128,32,256]{2,1,0:T(8,128)} %copy.213), calls=%async_computation.21 | async-start | bytes 8388608 | tf_op jit(solution)/shard_map/all_to_all | solution.py:80
  2243.9 98.6 %all-to-all-start.20 = ((f32[128,32,256]{2,1,0:T(8,128)}), f32[128,32,256]{2,1,0:T(8,128)}, u32[]{:S(2)}, u32[]{:S(2)}) async-start(f32[128,32,256]{2,1,0:T(8,128)} %copy.210), calls=%async_computation.20 | async-start | bytes 8388608 | tf_op jit(solution)/shard_map/all_to_all | solution.py:79
  2248.5 220.8 %all-reduce.4.cloned.1.call-start = ((), (), s32[]{:S(2)}) async-start(), calls=%async_computation.22 | async-start | bytes 8388608 | tf_op jit(solution)/shard_map/psum | solution.py:112
  (37 other events, 203.3 us)
Sparse Core Ops, SparseCore 0:
  334.7 173.9 all-reduce.5
  2366.9 102.4 all-reduce.3
where the time goes:
time: 2490 us; the launch traced here: 2480 us
  waiting for transfers between devices  1670 us (67%)
  matrix products  297 us (12%)
  blocking collectives  196 us (8%)
  local copies, waits for them, and re-layouts  168 us (7%)
  starting transfers between devices  96 us (4%)
  other arithmetic  38.3 us (2%)
    dot_general x50, matrix products, along_axis(): jnp.einsum(einsum_forms[axis_index], values_in, table, precision=highest)  277 us
    all_to_all x3, waiting for transfers between devices, forward_transform(): lax.all_to_all(imag_part, 'brick', split_axis=1, concat_axis=0, tiled=True)  250 us
    all_to_all x3, waiting for transfers between devices, forward_transform(): lax.all_to_all(real_part, 'brick', split_axis=1, concat_axis=0, tiled=True)  229 us
    all_to_all x2, blocking collectives, forward_transform(): lax.all_to_all(depth_real, 'brick', split_axis=0, concat_axis=1, tiled=True)  196 us
    all_to_all x2, waiting for transfers between devices, inverse_transform(): lax.all_to_all(real_part, 'brick', split_axis=1, concat_axis=0, tiled=True)  178 us
    all_to_all x2, waiting for transfers between devices, inverse_transform(): lax.all_to_all(imag_part, 'brick', split_axis=1, concat_axis=0, tiled=True)  174 us
    all_to_all x3, waiting for transfers between devices, forward_transform(): lax.all_to_all(depth_imag, 'brick', split_axis=0, concat_axis=1, tiled=True)  159 us
    all_to_all x2, waiting for transfers between devices, inverse_transform(): lax.all_to_all(imag_part, 'brick', split_axis=0, concat_axis=1, tiled=True)  158 us
  transfers between devices with their start and end apart: 22, of which 21 were waited for; matrix products, arithmetic and copies ran while one was open for 13% of the time, Pallas kernels for 0%

commit v1 on v0

--- a/solution.py
+++ b/solution.py
@@ -65,7 +65,12 @@
     )
     return (
         lax.all_to_all(depth_real, "brick", split_axis=0, concat_axis=1, tiled=True),
-        lax.all_to_all(depth_imag, "brick", split_axis=0, concat_axis=1, tiled=True),
+        jnp.concatenate(
+            lax.all_to_all(
+                jnp.stack(jnp.split(depth_imag, lax.axis_size("brick"), axis=0)), "brick", 0, 0
+            ),
+            axis=1,
+        ),
     )
 
 

time: 2490 us -> 2480 us (level)
  blocking collectives: 196 us -> 390 us
  waiting for transfers between devices: 1670 us -> 1490 us
    all_to_all x5 -> x1, waiting for transfers between devices: 333 us -> 74.3 us  [forward_transform(): lax.all_to_all(jnp.stack(jnp.split(depth_imag, lax.axis_size('brick'), ax...]
    all_to_all x2 -> x4, blocking collectives: 196 us -> 390 us  [the longest x2 195 us: forward_transform(): lax.all_to_all(jnp.stack(jnp.split(depth_imag, lax.axis_size('brick'), ax...]
    all_to_all x1 -> x3, waiting for transfers between devices: 74.3 us -> 154 us  [forward_transform(): lax.all_to_all(depth_real, 'brick', split_axis=0, concat_axis=1, tiled=True)]
  transfers between devices with their start and end apart: 22 -> 20, of which waited for: 21 -> 19; matrix products, arithmetic and copies ran while one was open for 13% -> 13% of each run, Pallas kernels for 0% -> 0%
where the time goes in v1:
time: 2480 us; the launch traced here: 2470 us
  waiting for transfers between devices  1490 us (60%)
  blocking collectives  390 us (16%)
  matrix products  297 us (12%)
  local copies, waits for them, and re-layouts  149 us (6%)
  starting transfers between devices  86.9 us (4%)
  other arithmetic  43.1 us (2%)
    dot_general x50, matrix products, along_axis(): jnp.einsum(einsum_forms[axis_index], values_in, table, precision=highest)  277 us
    all_to_all x3, waiting for transfers between devices, forward_transform(): lax.all_to_all(imag_part, 'brick', split_axis=1, concat_axis=0, tiled=True)  247 us
    all_to_all x3, waiting for transfers between devices, forward_transform(): lax.all_to_all(real_part, 'brick', split_axis=1, concat_axis=0, tiled=True)  229 us
    all_to_all x2, blocking collectives, forward_transform(): lax.all_to_all(jnp.stack(jnp.split(depth_imag, lax.axis_size('brick'), ax...  195 us
    all_to_all x2, blocking collectives, inverse_transform(): lax.all_to_all(imag_part, 'brick', split_axis=1, concat_axis=0, tiled=True)  195 us
    all_to_all x2, waiting for transfers between devices, inverse_transform(): lax.all_to_all(real_part, 'brick', split_axis=1, concat_axis=0, tiled=True)  178 us
    all_to_all x2, waiting for transfers between devices, inverse_transform(): lax.all_to_all(imag_part, 'brick', split_axis=0, concat_axis=1, tiled=True)  158 us
    all_to_all x3, waiting for transfers between devices, forward_transform(): lax.all_to_all(depth_real, 'brick', split_axis=0, concat_axis=1, tiled=True)  154 us
  transfers between devices with their start and end apart: 20, of which 19 were waited for; matrix products, arithmetic and copies ran while one was open for 13% of the time, Pallas kernels for 0%

profile of v1, /device:TPU:0, one launch (start us, length us, event | category | flops | bytes accessed | tf_op | source)
XLA Modules:
  0.0 2472.5 jit_solution(1218659012885809513)
XLA Ops:
  69.3 55.4 %all-to-all-done = f32[16,256,256]{2,0,1:T(8,128)} async-done(((f32[16,256,256]{2,0,1:T(8,128)}), f32[16,256,256]{2,0,1:T(8,128)}, u32[]{:S(2)}, u32[]{:S(2)}) %all-to-all-start) | async-done | bytes 4194336 | tf_op jit(solution)/shard_map/all_to_all | solution.py:51
  148.7 74.5 %all-to-all-done.5 = f32[16,256,256]{2,0,1:T(8,128)} async-done(((f32[16,256,256]{2,0,1:T(8,128)}), f32[16,256,256]{2,0,1:T(8,128)}, u32[]{:S(2)}, u32[]{:S(2)}) %all-to-all-start.5) | async-done | bytes 4194336 | tf_op jit(solution)/shard_map/all_to_all | solution.py:62
  250.9 70.9 %all-to-all-done.1 = f32[128,32,256]{2,1,0:T(8,128)} async-done(((f32[128,32,256]{2,1,0:T(8,128)}), f32[128,32,256]{2,1,0:T(8,128)}, u32[]{:S(2)}, u32[]{:S(2)}) %all-to-all-start.1) | async-done | bytes 4194336 | tf_op jit(solution)/shard_map/all_to_all | solution.py:55
  339.5 80.9 %all-to-all-done.6 = f32[16,256,256]{2,0,1:T(8,128)} async-done(((f32[16,256,256]{2,0,1:T(8,128)}), f32[16,256,256]{2,0,1:T(8,128)}, u32[]{:S(2)}, u32[]{:S(2)}) %all-to-all-start.6) | async-done | bytes 4194336 | tf_op jit(solution)/shard_map/all_to_all | solution.py:63
  441.3 67.4 %all-reduce.6.cloned.1.call-done = (f32[16,256,256]{2,1,0:T(8,128)}, f32[16,256,256]{2,1,0:T(8,128)}) async-done(((f32[16,256,256]{2,1,0:T(8,128)}, f32[16,256,256]{2,1,0:T(8,128)}), (f32[16,256,256]{2,1,0:T(8,128)}, f32[16,256,256]{2,1,0:T(8,128)})) %all-reduce.6.cloned.1.call-update) | async-done | bytes 8388624 | tf_op jit(solution)/shard_map/psum | solution.py:104
  558.3 77.3 %all-to-all-done.2 = f32[16,256,256]{2,0,1:T(8,128)} async-done(((f32[16,256,256]{2,0,1:T(8,128)}), f32[16,256,256]{2,0,1:T(8,128)}, u32[]{:S(2)}, u32[]{:S(2)}) %all-to-all-start.2) | async-done | bytes 4194336 | tf_op jit(solution)/shard_map/all_to_all | solution.py:62
  657.4 77.1 %all-to-all-done.3 = f32[16,256,256]{2,0,1:T(8,128)} async-done(((f32[16,256,256]{2,0,1:T(8,128)}), f32[16,256,256]{2,0,1:T(8,128)}, u32[]{:S(2)}, u32[]{:S(2)}) %all-to-all-start.3) | async-done | bytes 4194336 | tf_op jit(solution)/shard_map/all_to_all | solution.py:63
  759.1 74.3 %all-to-all-done.9 = f32[8,16,32,256]{3,1,2,0:T(8,128)} async-done(((f32[8,16,32,256]{3,1,2,0:T(8,128)}), f32[8,16,32,256]{3,1,2,0:T(8,128)}, u32[]{:S(2)}, u32[]{:S(2)}) %all-to-all-start.9) | async-done | bytes 4194336 | tf_op jit(solution)/shard_map/all_to_all | solution.py:69
  855.1 77.1 %all-to-all-done.4 = f32[128,32,256]{2,1,0:T(8,128)} async-done(((f32[128,32,256]{2,1,0:T(8,128)}), f32[128,32,256]{2,1,0:T(8,128)}, u32[]{:S(2)}, u32[]{:S(2)}) %all-to-all-start.4) | async-done | bytes 4194336 | tf_op jit(solution)/shard_map/all_to_all | solution.py:67
  932.2 97.6 %all_to_all.339 = f32[8,16,32,256]{3,1,2,0:T(8,128)S(1)} all-to-all(f32[8,16,32,256]{3,1,2,0:T(8,128)} %fusion.86), channel_id=1, replica_groups=mesh['view'=4,'brick'=8] {'brick'}, dimensions={0} | all-to-all | bytes 8388608 | tf_op jit(solution)/shard_map/all_to_all | solution.py:69
  1029.8 13.0 multiply_subtract_fusion.1
  1042.8 97.3 %all_to_all.340 = f32[16,256,256]{2,0,1:T(8,128)} all-to-all(f32[16,256,256]{2,0,1:T(8,128)S(1)} %bitcast.455), channel_id=1, replica_groups=mesh['view'=4,'brick'=8] {'brick'}, dimensions={1} | all-to-all | bytes 8388608 | tf_op jit(solution)/shard_map/all_to_all | solution.py:80
  1149.9 89.2 %all-to-all-done.10 = f32[16,256,256]{2,0,1:T(8,128)} async-done(((f32[16,256,256]{2,0,1:T(8,128)}), f32[16,256,256]{2,0,1:T(8,128)}, u32[]{:S(2)}, u32[]{:S(2)}) %all-to-all-start.10) | async-done | bytes 4194336 | tf_op jit(solution)/shard_map/all_to_all | solution.py:79
  1274.9 79.3 %all-to-all-done.13 = f32[128,32,256]{2,1,0:T(8,128)} async-done(((f32[128,32,256]{2,1,0:T(8,128)}), f32[128,32,256]{2,1,0:T(8,128)}, u32[]{:S(2)}, u32[]{:S(2)}) %all-to-all-start.13) | async-done | bytes 4194336 | tf_op jit(solution)/shard_map/all_to_all | solution.py:85
  1375.8 76.9 %all-to-all-done.12 = f32[128,32,256]{2,1,0:T(8,128)} async-done(((f32[128,32,256]{2,1,0:T(8,128)}), f32[128,32,256]{2,1,0:T(8,128)}, u32[]{:S(2)}, u32[]{:S(2)}) %all-to-all-start.12) | async-done | bytes 4194336 | tf_op jit(solution)/shard_map/all_to_all | solution.py:84
  1519.5 77.4 %all-to-all-done.14 = f32[16,256,256]{2,0,1:T(8,128)} async-done(((f32[16,256,256]{2,0,1:T(8,128)}), f32[16,256,256]{2,0,1:T(8,128)}, u32[]{:S(2)}, u32[]{:S(2)}) %all-to-all-start.14) | async-done | bytes 4194336 | tf_op jit(solution)/shard_map/all_to_all | solution.py:62
  1606.6 89.2 %all-to-all-done.15 = f32[16,256,256]{2,0,1:T(8,128)} async-done(((f32[16,256,256]{2,0,1:T(8,128)}), f32[16,256,256]{2,0,1:T(8,128)}, u32[]{:S(2)}, u32[]{:S(2)}) %all-to-all-start.15) | async-done | bytes 4194336 | tf_op jit(solution)/shard_map/all_to_all | solution.py:63
  1733.6 77.0 %all-to-all-done.16 = f32[128,32,256]{2,1,0:T(8,128)} async-done(((f32[128,32,256]{2,1,0:T(8,128)}), f32[128,32,256]{2,1,0:T(8,128)}, u32[]{:S(2)}, u32[]{:S(2)}) %all-to-all-start.16) | async-done | bytes 4194336 | tf_op jit(solution)/shard_map/all_to_all | solution.py:67
  1810.6 97.6 %all_to_all.341 = f32[8,16,32,256]{3,1,2,0:T(8,128)S(1)} all-to-all(f32[8,16,32,256]{3,1,2,0:T(8,128)} %fusion.70), channel_id=1, replica_groups=mesh['view'=4,'brick'=8] {'brick'}, dimensions={0} | all-to-all | bytes 8388608 | tf_op jit(solution)/shard_map/all_to_all | solution.py:69
  1921.2 97.3 %all_to_all.342 = f32[16,256,256]{2,0,1:T(8,128)} all-to-all(f32[16,256,256]{2,0,1:T(8,128)S(1)} %bitcast.454), channel_id=1, replica_groups=mesh['view'=4,'brick'=8] {'brick'}, dimensions={1} | all-to-all | bytes 8388608 | tf_op jit(solution)/shard_map/all_to_all | solution.py:80
  2028.1 89.2 %all-to-all-done.18 = f32[16,256,256]{2,0,1:T(8,128)} async-done(((f32[16,256,256]{2,0,1:T(8,128)}), f32[16,256,256]{2,0,1:T(8,128)}, u32[]{:S(2)}, u32[]{:S(2)}) %all-to-all-start.18) | async-done | bytes 4194336 | tf_op jit(solution)/shard_map/all_to_all | solution.py:79
  2153.2 79.2 %all-to-all-done.21 = f32[128,32,256]{2,1,0:T(8,128)} async-done(((f32[128,32,256]{2,1,0:T(8,128)}), f32[128,32,256]{2,1,0:T(8,128)}, u32[]{:S(2)}, u32[]{:S(2)}) %all-to-all-start.21) | async-done | bytes 4194336 | tf_op jit(solution)/shard_map/all_to_all | solution.py:85
  2253.9 77.1 %all-to-all-done.20 = f32[128,32,256]{2,1,0:T(8,128)} async-done(((f32[128,32,256]{2,1,0:T(8,128)}), f32[128,32,256]{2,1,0:T(8,128)}, u32[]{:S(2)}, u32[]{:S(2)}) %all-to-all-start.20) | async-done | bytes 4194336 | tf_op jit(solution)/shard_map/all_to_all | solution.py:84
  2355.2 102.6 %all-reduce.4.cloned.1.call-done = f32[16,256,256]{2,1,0:T(8,128)} async-done(((f32[16,256,256]{2,1,0:T(8,128)}), f32[16,256,256]{2,1,0:T(8,128)}) %all-reduce.4.cloned.1.call-update) | async-done | bytes 4194320 | tf_op jit(solution)/shard_map/psum | solution.py:117
  (214 shorter events, 562.3 us)
Async XLA Ops:
  24.3 100.4 %all-to-all-start = ((f32[16,256,256]{2,0,1:T(8,128)}), f32[16,256,256]{2,0,1:T(8,128)}, u32[]{:S(2)}, u32[]{:S(2)}) async-start(f32[16,256,256]{2,0,1:T(8,128)} %copy.150), calls=%async_computation | async-start | bytes 8388608 | tf_op jit(solution)/shard_map/all_to_all | solution.py:51
  30.6 10.7 copy-start.34
  41.3 15.7 copy-start.27
  124.7 98.6 %all-to-all-start.5 = ((f32[16,256,256]{2,0,1:T(8,128)}), f32[16,256,256]{2,0,1:T(8,128)}, u32[]{:S(2)}, u32[]{:S(2)}) async-start(f32[16,256,256]{2,0,1:T(8,128)} %copy.171), calls=%async_computation.5 | async-start | bytes 8388608 | tf_op jit(solution)/shard_map/all_to_all | solution.py:62
  223.3 98.6 %all-to-all-start.1 = ((f32[128,32,256]{2,1,0:T(8,128)}), f32[128,32,256]{2,1,0:T(8,128)}, u32[]{:S(2)}, u32[]{:S(2)}) async-start(f32[128,32,256]{2,1,0:T(8,128)} %copy.154), calls=%async_computation.1 | async-start | bytes 8388608 | tf_op jit(solution)/shard_map/all_to_all | solution.py:55
  227.8 11.0 copy-start.4
  321.9 98.6 %all-to-all-start.6 = ((f32[16,256,256]{2,0,1:T(8,128)}), f32[16,256,256]{2,0,1:T(8,128)}, u32[]{:S(2)}, u32[]{:S(2)}) async-start(f32[16,256,256]{2,0,1:T(8,128)} %copy.177), calls=%async_computation.6 | async-start | bytes 8388608 | tf_op jit(solution)/shard_map/all_to_all | solution.py:63
  326.4 182.2 %all-reduce.6.cloned.1.call-start = ((), (), s32[]{:S(2)}) async-start(), calls=%async_computation.23 | async-start | bytes 16777216 | tf_op jit(solution)/shard_map/psum | solution.py:104
  436.7 100.1 %all-to-all-start.7 = ((f32[128,32,256]{2,1,0:T(8,128)}), f32[128,32,256]{2,1,0:T(8,128)}, u32[]{:S(2)}, u32[]{:S(2)}) async-start(f32[128,32,256]{2,1,0:T(8,128)} %copy.179), calls=%async_computation.7 | async-start | bytes 8388608 | tf_op jit(solution)/shard_map/all_to_all | solution.py:67
  517.2 10.2 copy-start.5
  536.8 98.9 %all-to-all-start.2 = ((f32[16,256,256]{2,0,1:T(8,128)}), f32[16,256,256]{2,0,1:T(8,128)}, u32[]{:S(2)}, u32[]{:S(2)}) async-start(f32[16,256,256]{2,0,1:T(8,128)} %copy.158), calls=%async_computation.2 | async-start | bytes 8388608 | tf_op jit(solution)/shard_map/all_to_all | solution.py:62
  635.6 98.8 %all-to-all-start.3 = ((f32[16,256,256]{2,0,1:T(8,128)}), f32[16,256,256]{2,0,1:T(8,128)}, u32[]{:S(2)}, u32[]{:S(2)}) async-start(f32[16,256,256]{2,0,1:T(8,128)} %copy.162), calls=%async_computation.3 | async-start | bytes 8388608 | tf_op jit(solution)/shard_map/all_to_all | solution.py:63
  734.4 99.0 %all-to-all-start.9 = ((f32[8,16,32,256]{3,1,2,0:T(8,128)}), f32[8,16,32,256]{3,1,2,0:T(8,128)}, u32[]{:S(2)}, u32[]{:S(2)}) async-start(f32[8,16,32,256]{3,1,2,0:T(8,128)} %fusion.78), calls=%async_computation.9 | async-start | bytes 8388608 | tf_op jit(solution)/shard_map/all_to_all | solution.py:69
  833.4 98.8 %all-to-all-start.4 = ((f32[128,32,256]{2,1,0:T(8,128)}), f32[128,32,256]{2,1,0:T(8,128)}, u32[]{:S(2)}, u32[]{:S(2)}) async-start(f32[128,32,256]{2,1,0:T(8,128)} %copy.164), calls=%async_computation.4 | async-start | bytes 8388608 | tf_op jit(solution)/shard_map/all_to_all | solution.py:67
  1140.1 99.0 %all-to-all-start.10 = ((f32[16,256,256]{2,0,1:T(8,128)}), f32[16,256,256]{2,0,1:T(8,128)}, u32[]{:S(2)}, u32[]{:S(2)}) async-start(f32[16,256,256]{2,0,1:T(8,128)} %bitcast.453), calls=%async_computation.10 | async-start | bytes 8388608 | tf_op jit(solution)/shard_map/all_to_all | solution.py:79
  1255.4 98.8 %all-to-all-start.13 = ((f32[128,32,256]{2,1,0:T(8,128)}), f32[128,32,256]{2,1,0:T(8,128)}, u32[]{:S(2)}, u32[]{:S(2)}) async-start(f32[128,32,256]{2,1,0:T(8,128)} %copy.189), calls=%async_computation.13 | async-start | bytes 8388608 | tf_op jit(solution)/shard_map/all_to_all | solution.py:85
  1354.1 98.6 %all-to-all-start.12 = ((f32[128,32,256]{2,1,0:T(8,128)}), f32[128,32,256]{2,1,0:T(8,128)}, u32[]{:S(2)}, u32[]{:S(2)}) async-start(f32[128,32,256]{2,1,0:T(8,128)} %copy.186), calls=%async_computation.12 | async-start | bytes 8388608 | tf_op jit(solution)/shard_map/all_to_all | solution.py:84
  1498.4 98.6 %all-to-all-start.14 = ((f32[16,256,256]{2,0,1:T(8,128)}), f32[16,256,256]{2,0,1:T(8,128)}, u32[]{:S(2)}, u32[]{:S(2)}) async-start(f32[16,256,256]{2,0,1:T(8,128)} %copy.196), calls=%async_computation.14 | async-start | bytes 8388608 | tf_op jit(solution)/shard_map/all_to_all | solution.py:62
  1597.0 98.8 %all-to-all-start.15 = ((f32[16,256,256]{2,0,1:T(8,128)}), f32[16,256,256]{2,0,1:T(8,128)}, u32[]{:S(2)}, u32[]{:S(2)}) async-start(f32[16,256,256]{2,0,1:T(8,128)} %copy.200), calls=%async_computation.15 | async-start | bytes 8388608 | tf_op jit(solution)/shard_map/all_to_all | solution.py:63
  1711.7 99.0 %all-to-all-start.16 = ((f32[128,32,256]{2,1,0:T(8,128)}), f32[128,32,256]{2,1,0:T(8,128)}, u32[]{:S(2)}, u32[]{:S(2)}) async-start(f32[128,32,256]{2,1,0:T(8,128)} %copy.202), calls=%async_computation.16 | async-start | bytes 8388608 | tf_op jit(solution)/shard_map/all_to_all | solution.py:67
  2018.5 98.7 %all-to-all-start.18 = ((f32[16,256,256]{2,0,1:T(8,128)}), f32[16,256,256]{2,0,1:T(8,128)}, u32[]{:S(2)}, u32[]{:S(2)}) async-start(f32[16,256,256]{2,0,1:T(8,128)} %bitcast.452), calls=%async_computation.18 | async-start | bytes 8388608 | tf_op jit(solution)/shard_map/all_to_all | solution.py:79
  2133.4 99.0 %all-to-all-start.21 = ((f32[128,32,256]{2,1,0:T(8,128)}), f32[128,32,256]{2,1,0:T(8,128)}, u32[]{:S(2)}, u32[]{:S(2)}) async-start(f32[128,32,256]{2,1,0:T(8,128)} %copy.212), calls=%async_computation.21 | async-start | bytes 8388608 | tf_op jit(solution)/shard_map/all_to_all | solution.py:85
  2232.4 98.6 %all-to-all-start.20 = ((f32[128,32,256]{2,1,0:T(8,128)}), f32[128,32,256]{2,1,0:T(8,128)}, u32[]{:S(2)}, u32[]{:S(2)}) async-start(f32[128,32,256]{2,1,0:T(8,128)} %copy.209), calls=%async_computation.20 | async-start | bytes 8388608 | tf_op jit(solution)/shard_map/all_to_all | solution.py:84
  2237.0 220.9 %all-reduce.4.cloned.1.call-start = ((), (), s32[]{:S(2)}) async-start(), calls=%async_computation.22 | async-start | bytes 8388608 | tf_op jit(solution)/shard_map/psum | solution.py:117
  (35 other events, 178.2 us)
Sparse Core Ops, SparseCore 0:
  334.7 173.9 all-reduce.5
  2355.3 102.4 all-reduce.3
